TPU v7x, 128 devices: a whole 4x4x4 slice. The times are simulated.
128 devices in a mesh: grp: 16 (over y, z), sub: 8 (over x, core).
Axes of the slice: x: 4, y: 4, z: 4, core: 2. Of those that a mesh axis runs over, the one named last changes fastest.
Arguments:
- loads: float32 [1024, 256, 384], P(('grp', 'sub')), may hold values from -60 to 60
- diagonal_blocks: bfloat16 [1024, 384, 384], P(('grp', 'sub')), may hold values from -1 to 4
- lower_coupling: bfloat16 [1024, 384, 384], P(('grp', 'sub')), may hold values from -0.15625 to 0.15625
- upper_coupling: bfloat16 [1024, 384, 384], P(('grp', 'sub')), may hold values from -0.15625 to 0.15625
- local_inverse: bfloat16 [3, 1024, 384, 384], P(None, ('grp', 'sub')), may hold values from -0.5 to 1
- deflation: bfloat16 [1024, 32, 384], P(('grp', 'sub')), may hold values from -0.29882812 to 0.29882812
- coarse_inverse: float32 [4096, 4096], P(('grp', 'sub')), may hold values from -1 to 2, as said below
- coarse_order: int32 [4096], replicated, may hold values from 0 to 4095, as said below
Outputs:
- solution: float32 [1024, 256, 384], P(('grp', 'sub'))
- final_residual: float32 [1024, 256, 384], P(('grp', 'sub'))
- relative_residual: float32 [256], replicated
Inputs may be any that keep to these rules, and one draw needn't show every extreme that they name: `coarse_order`: each of 0 to 4095 once. coarse_inverse with its columns put back in coarse numbering is symmetric.
All inputs are finite; a program needn't handle non-finite values.
Results may differ from a plain program's by a relative error of at most 0.008.
Values may be sent and summed in bfloat16 or wider, within the bound.
A program may use at most 128 MiB of HBM per device.

v0:
```python
import jax
import jax.numpy as jnp
from jax import lax
from jax.sharding import PartitionSpec as P


def with_halo(cells, sides, width):
    for axis, dim in sides:
        count = lax.axis_size(axis)
        ends = count - 1
        head = lax.slice_in_dim(cells, 0, width, axis=dim)
        tail = lax.slice_in_dim(cells, cells.shape[dim] - width, cells.shape[dim], axis=dim)
        cells = jnp.concatenate(
            [
                lax.ppermute(tail, axis, [(i, (i + 1) % count) for i in range(ends)]),
                cells,
                lax.ppermute(head, axis, [((i + 1) % count, i) for i in range(ends)]),
            ],
            axis=dim,
        )
    return cells


def banded(padded, left_blocks, centre_blocks, right_blocks):
    summed = jnp.einsum(
        "lkw,lwv->lkv", padded[:-2], left_blocks, preferred_element_type=jnp.float32
    )
    summed = summed + jnp.einsum(
        "lkw,lwv->lkv", padded[1:-1], centre_blocks, preferred_element_type=jnp.float32
    )
    return summed + jnp.einsum(
        "lkw,lwv->lkv", padded[2:], right_blocks, preferred_element_type=jnp.float32
    )


def total_squares(field):
    return lax.psum(jnp.sum(field * field, axis=(0, 2)), ("grp", "sub"))


def project(first, second):
    return lax.psum(jnp.sum(first * second, axis=(0, 2)), ("grp", "sub"))


def local(
    loads,
    diagonal_blocks,
    lower_coupling,
    upper_coupling,
    local_inverse,
    deflation,
    coarse_inverse,
    coarse_order,
):

    def coarse_solve(coefficients):
        grouped = lax.all_gather(coefficients, "sub", axis=0, tiled=True)
        gathered = lax.all_gather(grouped, "grp", axis=0, tiled=True)
        picked = jnp.take(gathered, coarse_order, axis=0)
        return jnp.dot(
            coarse_inverse,
            picked,
            precision=lax.Precision.HIGHEST,
            preferred_element_type=jnp.float32,
        )

    def precondition(field):
        rounded = field.astype(jnp.bfloat16)
        padded = with_halo(rounded, ((("grp", "sub"), 0),), 1)
        coefficients = jnp.einsum(
            "liw,lkw->ik", deflation, rounded, preferred_element_type=jnp.float32
        )
        solved_half = coarse_solve(coefficients).astype(jnp.bfloat16)
        local_part = banded(padded, local_inverse[0], local_inverse[1], local_inverse[2])
        return local_part + jnp.einsum(
            "ik,liw->lkw", solved_half, deflation, preferred_element_type=jnp.float32
        )

    def operate(field):
        rounded = field.astype(jnp.bfloat16)
        padded = with_halo(rounded, ((("grp", "sub"), 0),), 1)
        return banded(padded, lower_coupling, diagonal_blocks, upper_coupling)

    initial_norm = jnp.sqrt(total_squares(loads))
    basis_one = loads / initial_norm[None, :, None]
    precond_one = precondition(basis_one)
    image_one = operate(precond_one)
    entry_11 = project(basis_one, image_one)
    remainder_one = image_one - entry_11[None, :, None] * basis_one
    entry_21 = jnp.sqrt(total_squares(remainder_one))
    basis_two = remainder_one / entry_21[None, :, None]
    precond_two = precondition(basis_two)
    image_two = operate(precond_two)
    entry_12 = project(basis_one, image_two)
    partial_image = image_two - entry_12[None, :, None] * basis_one
    entry_22 = project(basis_two, partial_image)
    remainder_two = partial_image - entry_22[None, :, None] * basis_two
    entry_32 = jnp.sqrt(total_squares(remainder_two))
    minor_12 = entry_11 * entry_22 - entry_21 * entry_12
    minor_13 = entry_11 * entry_32
    minor_23 = entry_21 * entry_32
    determinant = minor_12 * minor_12 + minor_13 * minor_13 + minor_23 * minor_23
    gram_11 = entry_11 * entry_11 + entry_21 * entry_21
    gram_12 = entry_11 * entry_12 + entry_21 * entry_22
    gram_22 = entry_12 * entry_12 + entry_22 * entry_22 + entry_32 * entry_32
    right_one = initial_norm * entry_11
    right_two = initial_norm * entry_12
    weight_one = (gram_22 * right_one - gram_12 * right_two) / determinant
    weight_two = (gram_11 * right_two - gram_12 * right_one) / determinant
    solution = weight_one[None, :, None] * precond_one + weight_two[None, :, None] * precond_two
    final_residual = (
        loads - weight_one[None, :, None] * image_one - weight_two[None, :, None] * image_two
    )
    error_one = initial_norm - entry_11 * weight_one - entry_12 * weight_two
    error_two = -(entry_21 * weight_one + entry_22 * weight_two)
    error_three = -entry_32 * weight_two
    relative_residual = (
        error_one * error_one + error_two * error_two + error_three * error_three
    ) / (initial_norm * initial_norm)
    return (solution, final_residual, relative_residual)


def solution(mesh):
    return jax.shard_map(
        local,
        mesh=mesh,
        in_specs=(
            P(("grp", "sub"), None, None),
            P(("grp", "sub"), None, None),
            P(("grp", "sub"), None, None),
            P(("grp", "sub"), None, None),
            P(None, ("grp", "sub"), None, None),
            P(("grp", "sub"), None, None),
            P(("grp", "sub"), None),
            P(),
        ),
        out_specs=(P(("grp", "sub"), None, None), P(("grp", "sub"), None, None), P()),
        check_vma=False,
    )
```

profile of v0, /device:TPU:0, one launch (start us, length us, event | category | flops | bytes accessed | tf_op | source)
XLA Modules:
  0.0 661.1 jit_solution(391356449613514710)
XLA Ops:
  7.2 2.3 multiply_reduce_fusion.5
  9.6 68.2 %psum.42 = f32[256]{0:T(256)S(1)} all-reduce(f32[256]{0:T(256)S(1)} %multiply_reduce_fusion.5), channel_id=1, replica_groups=mesh['grp'=16,'sub'=8] {'grp','sub'}, use_global_device_ids=true, to_apply=%region_1.0 | all-reduce | flops 256 | bytes 2048 | tf_op jit(solution)/shard_map/psum | solution.py:37
  77.8 2.2 fusion.89
  80.0 1.2 copy-done.6
  81.8 13.9 %all_gather.12 = f32[256,256]{1,0:T(8,128)} all-gather(f32[32,256]{1,0:T(8,128)S(1)} %convolution_bitcast_fusion.1), channel_id=1, replica_groups=mesh['grp'=16,'sub'=8] {'sub'}, dimensions={0}, use_global_device_ids=true | all-gather | bytes 294912 | tf_op jit(solution)/shard_map/all_gather | solution.py:56
  95.8 1.1 fusion.94
  96.8 1.3 collective-permute-start.1
  98.1 3.0 collective-permute-start
  101.2 5.2 fusion.10
  106.4 4.5 fusion.14
  110.9 33.4 %all-gather.3.cloned.1.call-done = f32[4096,256]{1,0:T(8,128)} async-done(((f32[256,256]{1,0:T(8,128)}), f32[4096,256]{1,0:T(8,128)}) %all-gather.3.cloned.1.call-update) | async-done | bytes 4194320 | tf_op jit(solution)/shard_map/all_gather | solution.py:57
  144.2 18.3 %gather_fusion = f32[4096,256]{1,0:T(8,128)} fusion(f32[4096,256]{1,0:T(8,128)} %all-gather.3.cloned.1.call-done, s32[4096]{0:T(1024)S(1)} %fusion.78), kind=kCustom, calls=%fused_computation.clone | custom fusion | bytes 8404992 | tf_op jit(solution)/shard_map/jit(_take)/gather | solution.py:58
  162.6 4.6 fusion.75
  167.8 4.9 fusion.95
  172.8 1.3 collective-permute-start.3
  174.1 3.4 collective-permute-start.2
  177.5 1.1 fusion.98
  178.6 1.1 fusion.36
  179.7 0.7 copy-done.1
  180.5 3.4 multiply_reduce_fusion.4
  183.8 72.2 %psum.43 = f32[256]{0:T(256)S(1)} all-reduce(f32[256]{0:T(256)S(1)} %get-tuple-element.21), channel_id=1, replica_groups=mesh['grp'=16,'sub'=8] {'grp','sub'}, use_global_device_ids=true, to_apply=%region_3.5 | all-reduce | flops 256 | bytes 2048 | tf_op jit(solution)/shard_map/psum | solution.py:41
  256.1 3.5 multiply_reduce_fusion.3
  259.6 64.8 %psum.44 = f32[256]{0:T(256)S(1)} all-reduce(f32[256]{0:T(256)S(1)} %multiply_reduce_fusion.3), channel_id=1, replica_groups=mesh['grp'=16,'sub'=8] {'grp','sub'}, use_global_device_ids=true, to_apply=%region_5.7 | all-reduce | flops 256 | bytes 2048 | tf_op jit(solution)/shard_map/psum | solution.py:37
  324.4 5.4 fusion.90
  329.8 1.2 copy-done.3
  331.5 13.9 %all_gather.14 = f32[256,256]{1,0:T(8,128)} all-gather(f32[32,256]{1,0:T(8,128)S(1)} %convolution_bitcast_fusion), channel_id=1, replica_groups=mesh['grp'=16,'sub'=8] {'sub'}, dimensions={0}, use_global_device_ids=true | all-gather | bytes 294912 | tf_op jit(solution)/shard_map/all_gather | solution.py:56
  345.4 1.1 fusion.92
  346.5 2.4 collective-permute-start.4
  348.9 4.9 fusion.8
  353.8 1.5 collective-permute-start.5
  355.3 4.5 fusion.12
  359.8 35.0 %all-gather.5.cloned.1.call-done = f32[4096,256]{1,0:T(8,128)} async-done(((f32[256,256]{1,0:T(8,128)}), f32[4096,256]{1,0:T(8,128)}) %all-gather.5.cloned.1.call-update) | async-done | bytes 4194320 | tf_op jit(solution)/shard_map/all_gather | solution.py:57
  394.9 18.3 %gather_fusion.1 = f32[4096,256]{1,0:T(8,128)} fusion(f32[4096,256]{1,0:T(8,128)} %all-gather.5.cloned.1.call-done, s32[4096]{0:T(1024)S(1)} %fusion.78), kind=kCustom, calls=%fused_computation.1.clone | custom fusion | bytes 8404992 | tf_op jit(solution)/shard_map/jit(_take)/gather | solution.py:58
  413.2 4.6 fusion.72
  418.4 4.9 fusion.96
  423.4 1.9 collective-permute-start.6
  425.3 1.1 fusion.100
  426.4 1.6 collective-permute-start.7
  428.0 1.1 fusion.54
  429.1 2.1 collective-permute-done.7
  431.2 3.4 multiply_reduce_fusion.2
  434.6 73.5 %psum.45 = f32[256]{0:T(256)S(1)} all-reduce(f32[256]{0:T(256)S(1)} %get-tuple-element.25), channel_id=1, replica_groups=mesh['grp'=16,'sub'=8] {'grp','sub'}, use_global_device_ids=true, to_apply=%region_7.9 | all-reduce | flops 256 | bytes 2048 | tf_op jit(solution)/shard_map/psum | solution.py:41
  508.2 4.5 multiply_reduce_fusion.1
  512.6 63.8 %psum.46 = f32[256]{0:T(256)S(1)} all-reduce(f32[256]{0:T(256)S(1)} %multiply_reduce_fusion.1), channel_id=1, replica_groups=mesh['grp'=16,'sub'=8] {'grp','sub'}, use_global_device_ids=true, to_apply=%region_9.11 | all-reduce | flops 256 | bytes 2048 | tf_op jit(solution)/shard_map/psum | solution.py:41
  576.4 4.7 multiply_reduce_fusion
  581.1 62.7 %psum.47 = f32[256]{0:T(256)S(1)} all-reduce(f32[256]{0:T(256)S(1)} %multiply_reduce_fusion), channel_id=1, replica_groups=mesh['grp'=16,'sub'=8] {'grp','sub'}, use_global_device_ids=true, to_apply=%region_11.13 | all-reduce | flops 256 | bytes 2048 | tf_op jit(solution)/shard_map/psum | solution.py:37
  643.8 0.6 multiply_divide_fusion
  644.4 9.9 %multiply_subtract_fusion = (f32[8,256,384]{2,1,0:T(8,128)}, f32[8,256,384]{2,1,0:T(8,128)}) fusion(f32[8,256,384]{2,1,0:T(8,128)} %get-tuple-element.26, f32[8,256,384]{2,1,0:T(8,128)} %param.10, f32[8,256,384]{2,1,0:T(8,128)} %get-tuple-element.22, f32[256]{0:T(256)S(1)} %get-tuple-element.6, f32[256]{0:T(256)S(1)} %get-tuple-element.5, ...), kind=kLoop, calls=%fused_computation.8 | loop fusion | flops 5505024 | bytes 22022144 | tf_op jit(solution)/shard_map/sub | solution.py:111
  (58 shorter events, 2.6 us)
Async XLA Ops:
  7.2 172.6 %copy-start = (bf16[8,384,384]{2,1,0:T(8,128)(2,1)S(1)}, bf16[8,384,384]{2,1,0:T(8,128)(2,1)}, u32[]{:S(2)}) copy-start(bf16[8,384,384]{2,1,0:T(8,128)(2,1)} %param.13) | copy-start | bytes 7077892
  7.2 137.1 %all-gather.3.cloned.1.call-start = ((), (), s32[]{:S(2)}) async-start(), calls=%async_computation | async-start | bytes 4456448 | tf_op jit(solution)/shard_map/all_gather | solution.py:57
  9.6 71.7 %copy-start.13 = (bf16[8,32,384]{2,1,0:T(8,128)(2,1)S(1)}, bf16[8,32,384]{2,1,0:T(8,128)(2,1)}, u32[]{:S(2)}) copy-start(bf16[8,32,384]{2,1,0:T(8,128)(2,1)} %param.15) | copy-start | bytes 589828
  77.8 23.4 %copy-start.15 = (s32[4096]{0:T(1024)S(1)}, s32[4096]{0:T(1024)}, u32[]{:S(2)}) copy-start(s32[4096]{0:T(1024)} %param.17) | copy-start | bytes 49156
  80.0 1.2 copy-start.6
  95.7 299.1 %all-gather.5.cloned.1.call-start = ((), (), s32[]{:S(2)}) async-start(), calls=%async_computation.1 | async-start | bytes 4456448 | tf_op jit(solution)/shard_map/all_gather | solution.py:57
  96.8 71.0 %collective-permute-start.1 = (bf16[1,256,384]{2,1,0:T(8,128)(2,1)S(1)}, bf16[1,256,384]{2,1,0:T(8,128)(2,1)S(1)}, u32[]{:S(2)}, u32[]{:S(2)}) collective-permute-start(bf16[1,256,384]{2,1,0:T(8,128)(2,1)S(1)} %get-tuple-element.15), channel_id=1, source_target_pairs={{1,0},{2,1},{3,2},{4,3},{5,4},{6,5},{7,6},{8,7},{9,8},{10,9},{11,1... | collective-permute-start | bytes 589832 | tf_op jit(solution)/shard_map/ppermute | solution.py:17
  98.1 8.3 %collective-permute-start = (bf16[1,256,384]{2,1,0:T(8,128)(2,1)S(1)}, bf16[1,256,384]{2,1,0:T(8,128)(2,1)S(1)}, u32[]{:S(2)}, u32[]{:S(2)}) collective-permute-start(bf16[1,256,384]{2,1,0:T(8,128)(2,1)S(1)} %get-tuple-element.16), channel_id=1, source_target_pairs={{0,1},{1,2},{2,3},{3,4},{4,5},{5,6},{6,7},{7,8},{8,9},{9,10},{10,1... | collective-permute-start | bytes 589832 | tf_op jit(solution)/shard_map/ppermute | solution.py:15
  101.2 5.2 copy-start.7
  110.9 51.7 %copy-start.14 = (f32[32,4096]{1,0:T(8,128)S(1)}, f32[32,4096]{1,0:T(8,128)}, u32[]{:S(2)}) copy-start(f32[32,4096]{1,0:T(8,128)} %param.16) | copy-start | bytes 1572868
  162.5 5.3 copy-start.8
  162.5 5.3 copy-start.12
  162.5 5.3 copy-start.19
  167.8 9.7 %copy-start.9 = (bf16[8,384,384]{2,1,0:T(8,128)(2,1)S(1)}, bf16[8,384,384]{2,1,0:T(8,128)(2,1)}, u32[]{:S(2)}) copy-start(bf16[8,384,384]{2,1,0:T(8,128)(2,1)} %param.11) | copy-start | bytes 7077892
  172.8 7.0 %collective-permute-start.3 = (bf16[1,256,384]{2,1,0:T(8,128)(2,1)S(1)}, bf16[1,256,384]{2,1,0:T(8,128)(2,1)S(1)}, u32[]{:S(2)}, u32[]{:S(2)}) collective-permute-start(bf16[1,256,384]{2,1,0:T(8,128)(2,1)S(1)} %get-tuple-element.13), channel_id=1, source_target_pairs={{1,0},{2,1},{3,2},{4,3},{5,4},{6,5},{7,6},{8,7},{9,8},{10,9},{11,1... | collective-permute-start | bytes 589832 | tf_op jit(solution)/shard_map/ppermute | solution.py:17
  174.1 4.5 copy-start.16
  174.1 4.5 collective-permute-start.2
  178.6 1.9 copy-start.1
  329.8 1.2 copy-start.3
  346.5 8.8 %copy-start.4 = (bf16[8,256,384]{2,1,0:T(8,128)(2,1)S(1)}, bf16[8,256,384]{2,1,0:T(8,128)(2,1)}, u32[]{:S(2)}) copy-start(bf16[8,256,384]{2,1,0:T(8,128)(2,1)} %copy-done.3) | copy-start | bytes 4718596
  346.5 8.8 %collective-permute-start.4 = (bf16[1,256,384]{2,1,0:T(8,128)(2,1)S(1)}, bf16[1,256,384]{2,1,0:T(8,128)(2,1)S(1)}, u32[]{:S(2)}, u32[]{:S(2)}) collective-permute-start(bf16[1,256,384]{2,1,0:T(8,128)(2,1)S(1)} %get-tuple-element.12), channel_id=1, source_target_pairs={{0,1},{1,2},{2,3},{3,4},{4,5},{5,6},{6,7},{7,8},{8,9},{9,10},{10,1... | collective-permute-start | bytes 589832 | tf_op jit(solution)/shard_map/ppermute | solution.py:15
  353.8 64.6 %collective-permute-start.5 = (bf16[1,256,384]{2,1,0:T(8,128)(2,1)S(1)}, bf16[1,256,384]{2,1,0:T(8,128)(2,1)S(1)}, u32[]{:S(2)}, u32[]{:S(2)}) collective-permute-start(bf16[1,256,384]{2,1,0:T(8,128)(2,1)S(1)} %get-tuple-element.11), channel_id=1, source_target_pairs={{1,0},{2,1},{3,2},{4,3},{5,4},{6,5},{7,6},{8,7},{9,8},{10,9},{11,1... | collective-permute-start | bytes 589832 | tf_op jit(solution)/shard_map/ppermute | solution.py:17
  413.2 5.2 copy-start.5
  413.2 5.3 copy-start.11
  413.2 5.3 copy-start.18
  418.4 6.9 %copy-start.10 = (bf16[8,384,384]{2,1,0:T(8,128)(2,1)S(1)}, bf16[8,384,384]{2,1,0:T(8,128)(2,1)}, u32[]{:S(2)}) copy-start(bf16[8,384,384]{2,1,0:T(8,128)(2,1)} %param.11) | copy-start | bytes 7077892
  423.4 4.6 copy-start.17
  423.4 4.6 collective-permute-start.6
  426.4 4.9 copy-start.2
  426.4 4.8 collective-permute-start.7
Sparse Core Ops, SparseCore 0:
  95.8 48.3 all-gather.2
  345.5 49.2 all-gather.4
where the time goes:
time: 663 us; the launch traced here: 661 us
  blocking collectives  433 us (65%)
  waiting for transfers between devices  70.6 us (11%)
  matrix products  51.5 us (8%)
  local copies, waits for them, and re-layouts  42 us (6%)
  other arithmetic  33.1 us (5%)
  starting transfers between devices  16.4 us (2%)
  between operations  14.5 us (2%)
    psum x3, blocking collectives, project(): return lax.psum(jnp.sum(first * second, axis=(0, 2)), ('grp', 'sub'))  210 us
    psum x3, blocking collectives, total_squares(): return lax.psum(jnp.sum(field * field, axis=(0, 2)), ('grp', 'sub'))  196 us
    all_gather x2, waiting for transfers between devices, coarse_solve(): gathered = lax.all_gather(grouped, 'grp', axis=0, tiled=True)  68.4 us
    gather x2, local copies, waits for them, and re-layouts, coarse_solve(): picked = jnp.take(gathered, coarse_order, axis=0)  36.6 us
    all_gather x2, blocking collectives, coarse_solve(): grouped = lax.all_gather(coefficients, 'sub', axis=0, tiled=True)  27.9 us
    dot_general x4, matrix products, banded(): jnp.einsum('lkw,lwv->lkv', padded[2:], right_blocks, preferred_element_ty...  16.5 us
  transfers between devices with their start and end apart: 10, of which 3 were waited for; matrix products, arithmetic and copies ran while one was open for 11% of the time, Pallas kernels for 0%

commit v1 on v0

v1 whole, which is shorter than its diff:
```python
import jax
import jax.numpy as jnp
from jax import lax
from jax.experimental import pallas as pl
from jax.experimental.pallas import tpu as pltpu
from jax.sharding import PartitionSpec as P

MESH = pl.DeviceIdType.MESH
F32 = jnp.float32
BF16 = jnp.bfloat16

L = 8
K = 256
W = 384
NDEF = 32
SIDE = 4
SAME = SIDE * SIDE * SIDE * NDEF
NCOARSE = 2 * SAME
BAND = 3 * W
GATHER_PARTS = (
    ("xyz", 0, 16, 0, 256),
    ("yzx", 16, 32, 0, 128),
    ("zxy", 16, 32, 128, 256),
)


def lanes(plane):
    return pl.ds(pl.multiple_of(plane * W, W), W)


def kernel(
    loads_h, diagonal_h, lower_h, upper_h, local_h, deflation_h, inverse_h, order_h,
    solution_h, residual_h, relative_ref,
    v0, z0, u0, z1, u1, field0, field1, field2, field3, precond, coupling, vectors,
    own_rows, other_rows, split_rows, columns, order, place, gathered, partial, other_partial,
    gram, sums, slots,
    load_sem, vector_sem, block_sem, row_sem, out_sem,
    halo_send, halo_recv, gather_send, gather_recv, row_send, row_recv,
    partial_send, partial_recv, sum_send, sum_recv,
):
    grp = lax.axis_index("grp")
    sub = lax.axis_index("sub")
    y, z, x, core = grp // SIDE, grp % SIDE, sub // 2, sub % 2
    me = grp * 8 + sub
    before = (me + 127) % 128
    after = (me + 1) % 128
    before_id = (before // 8, before % 8)
    after_id = (after // 8, after % 8)
    core_id = (grp, x * 2 + 1 - core)
    place_of = {"x": x, "y": y, "z": z}

    def partner(axis, step):
        if axis == "x":
            return (grp, ((x + step) % SIDE) * 2 + core)
        if axis == "y":
            return (((y + step) % SIDE) * SIDE + z, sub)
        return (y * SIDE + (z + step) % SIDE, sub)

    def load_copy(plane):
        return pltpu.make_async_copy(loads_h.at[plane], v0.at[plane], load_sem.at[plane])

    def vector_copy(plane):
        return pltpu.make_async_copy(
            deflation_h.at[plane], vectors.at[:NDEF, lanes(plane)], vector_sem.at[plane]
        )

    block_copies = [
        pltpu.make_async_copy(source, target, block_sem.at[i])
        for i, (source, target) in enumerate([
            (local_h.at[0], precond.at[:, 0]),
            (local_h.at[1], precond.at[:, 1]),
            (local_h.at[2], precond.at[:, 2]),
            (lower_h, coupling.at[:, 0]),
            (diagonal_h, coupling.at[:, 1]),
            (upper_h, coupling.at[:, 2]),
        ])
    ]
    row_copy = pltpu.make_async_copy(inverse_h, own_rows, row_sem.at[0])
    order_copy = pltpu.make_async_copy(order_h, order, row_sem.at[1])
    for plane in (0, 7, 1, 2, 3, 4, 5, 6):
        load_copy(plane).start()
    for plane in range(L):
        vector_copy(plane).start()
    row_copy.start()
    order_copy.start()
    for copy in block_copies:
        copy.start()

    barrier = pltpu.get_barrier_semaphore()
    partners = [partner(axis, step) for axis in "xyz" for step in (1, 2, 3)]
    partners += [core_id, before_id, after_id]
    for device in partners:
        pl.semaphore_signal(barrier, inc=1, device_id=device, device_id_type=MESH)
    pl.semaphore_wait(barrier, len(partners))

    def remote(source, target, send, recv, device):
        return pltpu.make_async_remote_copy(
            src_ref=source, dst_ref=target, send_sem=send, recv_sem=recv,
            device_id=device, device_id_type=MESH,
        )

    row_exchange = remote(inverse_h, other_rows, row_send.at[0], row_recv.at[0], core_id)
    row_exchange.start()

    sends = [row_exchange]

    def halo_copies(field, which):
        return (
            remote(
                field.at[:, lanes(1)], field.at[:, lanes(L + 1)],
                halo_send.at[which, 0], halo_recv.at[which, 0], before_id,
            ),
            remote(
                field.at[:, lanes(L)], field.at[:, lanes(0)],
                halo_send.at[which, 1], halo_recv.at[which, 1], after_id,
            ),
        )

    def start_halo(field, which):
        for copy in halo_copies(field, which):
            copy.start()
            sends.append(copy)

    def finish_halo(field, which):
        for copy in halo_copies(field, which):
            copy.wait_recv()

        @pl.when(me == 0)
        def _():
            field[:, lanes(0)] = jnp.zeros((K, W), BF16)

        @pl.when(me == 127)
        def _():
            field[:, lanes(L + 1)] = jnp.zeros((K, W), BF16)

    def gather_copies(which, stage):
        found = []
        for part, (axes, row0, row1, lane0, lane1) in enumerate(GATHER_PARTS):
            done = axes[:stage]
            spot = tuple(slice(None) if name in done else place_of[name] for name in "yzx")
            block = gathered.at[(which,) + spot + (slice(row0, row1), slice(lane0, lane1))]
            for step in (1, 2, 3):
                found.append(remote(
                    block, block,
                    gather_send.at[which, part, stage, step - 1],
                    gather_recv.at[which, part, stage, step - 1],
                    partner(axes[stage], step),
                ))
        return found

    def start_gather(which, stage):
        copies = gather_copies(which, stage)
        for copy in copies:
            copy.start()
        sends.extend(copies)

    def finish_gather(which, stage):
        for copy in gather_copies(which, stage):
            copy.wait_recv()

    def coefficients(field, which):
        own = lax.dot_general(
            vectors[:NDEF], field[:, W:(L + 1) * W], (((1,), (1,)), ((), ())),
            preferred_element_type=F32,
        )
        gathered[which, y, z, x] = own.astype(BF16)

    def banded(field, blocks, plane):
        window = field[:, pl.ds(pl.multiple_of(plane * W, W), BAND)]
        return jnp.dot(
            window, blocks[plane].reshape(BAND, W), preferred_element_type=F32
        )

    def coarse_part(amounts, plane):
        return lax.dot_general(
            amounts, vectors[:, lanes(plane)], (((0,), (0,)), ((), ())),
            preferred_element_type=F32,
        )

    def finish_coarse(which):
        product = jnp.dot(
            columns[...], gathered[which].reshape(SAME, K), preferred_element_type=F32
        )
        both = product[:2 * NDEF] + product[2 * NDEF:]
        partial[which] = both
        exchange = remote(
            partial.at[which, NDEF:], other_partial.at[which],
            partial_send.at[which], partial_recv.at[which], core_id,
        )
        exchange.start()
        sends.append(exchange)
        exchange.wait_recv()
        total = partial[which, :NDEF] + other_partial[which]
        high = total.astype(BF16)
        low = (total - high.astype(F32)).astype(BF16)
        return jnp.concatenate([high, low], axis=0)

    def edge(i):
        return i * (L - 1)

    def round_load(plane):
        load_copy(plane).wait()
        field0[:, lanes(plane + 1)] = v0[plane].astype(BF16)

    round_load(0)
    round_load(7)
    start_halo(field0, 0)

    @pl.loop(1, L - 1)
    def _(plane):
        round_load(plane)

    @pl.loop(0, L)
    def _(plane):
        vector_copy(plane).wait()

    coefficients(field0, 0)
    start_gather(0, 0)
    vectors[NDEF:] = vectors[:NDEF]

    row_copy.wait()
    order_copy.wait()
    row_exchange.wait_recv()
    for i, rows in enumerate((own_rows, other_rows)):
        value = rows[...]
        high = value.astype(BF16)
        split_rows[i * NDEF:(i + 1) * NDEF] = high
        split_rows[(2 + i) * NDEF:(3 + i) * NDEF] = (value - high.astype(F32)).astype(BF16)
    unknown = order[...]
    chip, inside = unknown // (2 * NDEF), unknown % (2 * NDEF)
    mine = inside // NDEF == core
    place[...] = jnp.where(mine, chip * NDEF + inside % NDEF, -1)

    @pl.loop(0, SAME // 256)
    def _(block):
        base = block * 256
        total = jnp.zeros((4 * NDEF, 256), F32)
        for part in range(4):
            span = slice(part * 1024, (part + 1) * 1024)
            row = lax.broadcasted_iota(jnp.int32, (256, 1024), 0)
            hot = jnp.where(place[:, span] - base == row, 1.0, 0.0).astype(BF16)
            total += lax.dot_general(
                split_rows[:, span], hot, (((1,), (1,)), ((), ())), preferred_element_type=F32
            )
        columns[:, pl.ds(pl.multiple_of(base, 256), 256)] = total.astype(BF16)

    finish_gather(0, 0)
    start_gather(0, 1)
    for copy in block_copies[:3]:
        copy.wait()

    def precondition(field, result, which):
        @pl.loop(1, L - 1)
        def _(plane):
            result[plane] = banded(field, precond, plane)

        finish_gather(which, 1)
        start_gather(which, 2)
        finish_halo(field, which * 2)

        @pl.loop(0, 2)
        def _(i):
            result[edge(i)] = banded(field, precond, edge(i))

    def expand(result, field, which):
        finish_gather(which, 2)
        amounts = finish_coarse(which)

        def add(plane):
            total = result[plane] + coarse_part(amounts, plane)
            result[plane] = total
            field[:, lanes(plane + 1)] = total.astype(BF16)

        @pl.loop(0, 2)
        def _(i):
            add(edge(i))

        start_halo(field, which * 2 + 1)

        @pl.loop(1, L - 1)
        def _(plane):
            add(plane)

    def operate(field, result, which, rounded):
        def apply(plane):
            image = banded(field, coupling, plane)
            result[plane] = image
            if rounded is not None:
                rounded[:, lanes(plane + 1)] = image.astype(BF16)

        @pl.loop(1, L - 1)
        def _(plane):
            apply(plane)

        finish_halo(field, which * 2 + 1)

        @pl.loop(0, 2)
        def _(i):
            apply(edge(i))

    def inner_products(pairs):
        rows = 32

        @pl.loop(0, K // rows)
        def _(chunk):
            span = pl.ds(pl.multiple_of(chunk * rows, rows), rows)
            for column, first, second in pairs:
                total = jnp.zeros((rows, 128), F32)
                for plane in range(L):
                    for lane in range(0, W, 128):
                        total += (
                            first[plane, span, lane:lane + 128]
                            * second[plane, span, lane:lane + 128]
                        )
                gram[span, column:column + 1] = jnp.sum(total, axis=1, keepdims=True)

    precondition(field0, z0, 0)
    expand(z0, field1, 0)
    for copy in block_copies[3:]:
        copy.wait()
    operate(field1, u0, 0, field2)
    start_halo(field2, 2)
    coefficients(field2, 1)
    start_gather(1, 0)
    gram[...] = jnp.zeros((K, 128), F32)
    inner_products(((0, v0, v0), (1, v0, u0), (2, u0, u0)))
    finish_gather(1, 0)
    start_gather(1, 1)
    precondition(field2, z1, 1)
    expand(z1, field3, 1)
    operate(field3, u1, 1, None)
    inner_products(((3, v0, u1), (4, u0, u1), (5, u1, u1)))
    sums[...] = jnp.transpose(gram[...])[:8]

    pair = remote(sums, slots.at[0, 0], sum_send.at[0, 0], sum_recv.at[0, 0], core_id)
    pair.start()
    pair.wait()
    sums[...] = sums[...] + slots[0, 0]
    for stage, axis in ((1, "x"), (2, "y"), (3, "z")):
        spot = place_of[axis]
        slots[stage, spot] = sums[...]
        copies = [
            remote(
                slots.at[stage, spot], slots.at[stage, spot],
                sum_send.at[stage, step - 1], sum_recv.at[stage, step - 1],
                partner(axis, step),
            )
            for step in (1, 2, 3)
        ]
        for copy in copies:
            copy.start()
        for copy in copies:
            copy.wait()
        sums[...] = (slots[stage, 0] + slots[stage, 1]) + (slots[stage, 2] + slots[stage, 3])

    g00, g01, g11 = sums[0:1], sums[1:2], sums[2:3]
    g02, g12, g22 = sums[3:4], sums[4:5], sums[5:6]
    s0, s1, s2 = jnp.sqrt(g00), jnp.sqrt(g11), jnp.sqrt(g22)
    r01 = g01 / s0 / s1
    r02 = g02 / s0 / s2
    r11 = jnp.sqrt((1.0 - r01) * (1.0 + r01))
    r12 = (g12 / s1 / s2 - r01 * r02) / r11
    r22 = jnp.sqrt((1.0 - r02) * (1.0 + r02) - r12 * r12)
    n0 = r11 * r22
    n1 = r01 * r22
    n2 = r01 * r12 - r11 * r02
    share = n0 / (n0 * n0 + n1 * n1 + n2 * n2)
    relative_ref[...] = n0 * share
    scaled1 = -(share * n2) / r22
    weight1 = scaled1 * (s0 / s2)
    weight0 = (share * n1 - scaled1 * r12) / r11 * (s0 / s1)
    gram[...] = jnp.transpose(
        jnp.concatenate([weight0, weight1, jnp.zeros((126, K), F32)], axis=0)
    )

    def solution_copy(plane):
        return pltpu.make_async_copy(z0.at[plane], solution_h.at[plane], out_sem.at[0, plane])

    def residual_copy(plane):
        return pltpu.make_async_copy(v0.at[plane], residual_h.at[plane], out_sem.at[1, plane])

    @pl.loop(0, L)
    def _(plane):
        first = gram[:, 0:1]
        second = gram[:, 1:2]
        z0[plane] = first * z0[plane] + second * z1[plane]
        solution_copy(plane).start()
        v0[plane] = v0[plane] - first * u0[plane] - second * u1[plane]
        residual_copy(plane).start()

    for copy in sends:
        copy.wait_send()

    @pl.loop(0, L)
    def _(plane):
        solution_copy(plane).wait()
        residual_copy(plane).wait()


def local(
    loads, diagonal_blocks, lower_coupling, upper_coupling, local_inverse, deflation,
    coarse_inverse, coarse_order,
):
    hbm = pl.BlockSpec(memory_space=pl.ANY)
    field = pltpu.VMEM((L, K, W), F32)
    padded = pltpu.VMEM((K, (L + 2) * W), BF16)
    blocks = pltpu.VMEM((L, 3, W, W), BF16)
    dma = pltpu.SemaphoreType.DMA
    answer, residual, relative = pl.pallas_call(
        kernel,
        out_shape=(
            jax.ShapeDtypeStruct((L, K, W), F32),
            jax.ShapeDtypeStruct((L, K, W), F32),
            jax.ShapeDtypeStruct((1, K), F32),
        ),
        in_specs=[hbm] * 8,
        out_specs=(hbm, hbm, pl.BlockSpec(memory_space=pltpu.VMEM)),
        scratch_shapes=[
            field, field, field, field, field,
            padded, padded, padded, padded,
            blocks, blocks,
            pltpu.VMEM((2 * NDEF, L * W), BF16),
            pltpu.VMEM((NDEF, NCOARSE), F32),
            pltpu.VMEM((NDEF, NCOARSE), F32),
            pltpu.VMEM((4 * NDEF, NCOARSE), BF16),
            pltpu.VMEM((4 * NDEF, SAME), BF16),
            pltpu.VMEM((1, NCOARSE), jnp.int32),
            pltpu.VMEM((1, NCOARSE), jnp.int32),
            pltpu.VMEM((2, SIDE, SIDE, SIDE, NDEF, K), BF16),
            pltpu.VMEM((2, 2 * NDEF, K), F32),
            pltpu.VMEM((2, NDEF, K), F32),
            pltpu.VMEM((K, 128), F32),
            pltpu.VMEM((8, K), F32),
            pltpu.VMEM((4, SIDE, 8, K), F32),
            dma((L,)), dma((L,)), dma((6,)), dma((2,)), dma((2, L)),
            dma((4, 2)), dma((4, 2)), dma((2, 3, 3, 3)), dma((2, 3, 3, 3)),
            dma((1,)), dma((1,)), dma((2,)), dma((2,)), dma((4, 3)), dma((4, 3)),
        ],
        compiler_params=pltpu.CompilerParams(
            collective_id=0, has_side_effects=True, vmem_limit_bytes=60 * 2**20
        ),
        cost_estimate=pl.CostEstimate(
            flops=8 * 10**9, bytes_accessed=25 * 10**6, transcendentals=0
        ),
    )(
        loads, diagonal_blocks, lower_coupling, upper_coupling, local_inverse, deflation,
        coarse_inverse, coarse_order.reshape(1, NCOARSE),
    )
    return answer, residual, relative.reshape(K)


def solution(mesh):
    spread = P(("grp", "sub"))
    return jax.shard_map(
        local,
        mesh=mesh,
        in_specs=(
            spread, spread, spread, spread, P(None, ("grp", "sub")), spread, spread, P(),
        ),
        out_specs=(spread, spread, P()),
        check_vma=False,
    )
```

time: 663 us -> 87.6 us (0.13)
  blocking collectives: 433 us -> 0 us
  Pallas kernels: 0 us -> 80.7 us
  waiting for transfers between devices: 70.6 us -> 0 us
  matrix products: 51.5 us -> 0 us
  local copies, waits for them, and re-layouts: 42 us -> 6.17 us
  other arithmetic: 33.1 us -> 0 us
  starting transfers between devices: 16.4 us -> 0 us
  between operations: 14.5 us -> 0.65 us
    psum x6 -> x0, blocking collectives: 405 us -> none  [the longest x3 210 us: project(): return lax.psum(jnp.sum(first * second, axis=(0, 2)), ('grp', 'sub'))]
    pallas_call x0 -> x1, Pallas kernels: none -> 80.7 us  [local(): pl.pallas_call(kernel, out_shape=(jax.ShapeDtypeStruct((L, K, W), F32), j...]
    all_gather x2 -> x0, waiting for transfers between devices: 68.4 us -> none  [coarse_solve(): gathered = lax.all_gather(grouped, 'grp', axis=0, tiled=True)]
    dot_general x18 -> x0, matrix products: 51.5 us -> none  [the longest x4 16.5 us: banded(): jnp.einsum('lkw,lwv->lkv', padded[2:], right_blocks, preferred_element_ty...]
    gather x2 -> x0, local copies, waits for them, and re-layouts: 36.6 us -> none  [coarse_solve(): picked = jnp.take(gathered, coarse_order, axis=0)]
    all_gather x2 -> x0, blocking collectives: 27.9 us -> none  [coarse_solve(): grouped = lax.all_gather(coefficients, 'sub', axis=0, tiled=True)]
    ppermute x8 -> x0, starting transfers between devices: 16.3 us -> none  [the longest x4 10.7 us: with_halo(): lax.ppermute(tail, axis, [(i, (i + 1) % count) for i in range(ends)])]
    reduce_sum x4 -> x0, other arithmetic: 15 us -> none  [the longest x3 10.6 us: total_squares(): return lax.psum(jnp.sum(field * field, axis=(0, 2)), ('grp', 'sub'))]
  transfers between devices with their start and end apart: 10 -> 0, of which waited for: 3 -> 0; matrix products, arithmetic and copies ran while one was open for 11% -> 0% of each run, Pallas kernels for 0% -> 0%
where the time goes in v1:
time: 87.6 us; the launch traced here: 87.5 us
  Pallas kernels  80.7 us (92%)
  local copies, waits for them, and re-layouts  6.17 us (7%)
    pallas_call x1, Pallas kernels, local(): pl.pallas_call(kernel, out_shape=(jax.ShapeDtypeStruct((L, K, W), F32), j...  80.7 us
    unnamed x7, local copies, waits for them, and re-layouts  6.17 us

profile of v1, /device:TPU:0, one launch (start us, length us, event | category | flops | bytes accessed | tf_op | source)
XLA Modules:
  0.0 87.5 jit_solution(10064785101484161053)
XLA Ops:
  0.6 80.7 %shard_map.103 = (f32[8,256,384]{2,1,0:T(8,128)}, f32[8,256,384]{2,1,0:T(8,128)}, f32[1,256]{1,0:T(1,128)}) custom-call(f32[8,256,384]{2,1,0:T(8,128)} %loads_h.1, bf16[8,384,384]{2,1,0:T(8,128)(2,1)} %diagonal_h.1, bf16[8,384,384]{2,1,0:T(8,128)(2,1)} %lower_h.1, bf16[8,384,384]{2,1,0:T(8,128)(2,1)} %upper_h.1, bf16[3,8,384,384]{3,2,1,0:T(8,128)(2,1)} %local_h.1, ...), custom_call_target="tpu_custom_call" | custom-call | flops 8000000000 | bytes 25000000 | tf_op jit(solution)/shard_map/pallas_call | solution.py:409
  81.3 0.0 copy-start
  81.3 3.9 %copy.14 = f32[8,256,384]{2,1,0:T(8,128)} copy(f32[8,256,384]{2,1,0:T(8,128)} %get-tuple-element.12) | data formatting | bytes 6291456
  85.3 0.0 copy-done
  85.3 0.0 copy-start.1
  85.3 1.7 %copy.15 = f32[8,256,384]{2,1,0:T(8,128)} copy(f32[8,256,384]{2,1,0:T(8,128)S(1)} %copy-done) | data formatting | bytes 6291456
  86.9 0.0 copy-done.1
  87.0 0.6 copy.16
Async XLA Ops:
  81.3 3.9 %copy-start = (f32[8,256,384]{2,1,0:T(8,128)S(1)}, f32[8,256,384]{2,1,0:T(8,128)}, u32[]{:S(2)}) copy-start(f32[8,256,384]{2,1,0:T(8,128)} %get-tuple-element.13) | copy-start | bytes 9437188
  85.3 1.7 %copy-start.1 = (f32[1,256]{1,0:T(1,128)S(1)}, f32[1,256]{1,0:T(1,128)}, u32[]{:S(2)}) copy-start(f32[1,256]{1,0:T(1,128)} %get-tuple-element.8) | copy-start | bytes 3076

commit v2 on v1

v2 whole, which is shorter than its diff:
```python
import jax
import jax.numpy as jnp
from jax import lax
from jax.experimental import pallas as pl
from jax.experimental.pallas import tpu as pltpu
from jax.sharding import PartitionSpec as P

MESH = pl.DeviceIdType.MESH
F32 = jnp.float32
BF16 = jnp.bfloat16

L = 8
K = 256
W = 384
NDEF = 32
SIDE = 4
DEVICES = 128
SAME = SIDE * SIDE * SIDE * NDEF
NCOARSE = 2 * SAME
BAND = 3 * W
IMAGE_SCALE = 2.0 ** -24
GATHER_PARTS = (
    ("xyz", 0, 16, 0, 256),
    ("yzx", 16, 32, 0, 128),
    ("zxy", 16, 32, 128, 256),
)
NN = (((1,), (0,)), ((), ()))
NT = (((1,), (1,)), ((), ()))


def lanes(plane):
    return pl.ds(pl.multiple_of(plane * W, W), W)


def dot(first, second, form=NN, precision=None):
    return lax.dot_general(
        first, second, form, precision=precision, preferred_element_type=F32
    )


def two_terms(value):
    high = value.astype(BF16)
    return high, (value - high.astype(F32)).astype(BF16)


def kernel(
    loads_h, diagonal_h, lower_h, upper_h, local_h, deflation_h, inverse_h, order_h,
    solution_h, residual_h, relative_ref,
    v0, z0, u0, z1, u1, field0, field1, field2, field3, precond, coupling,
    padded_vectors, edge_vectors, expansion, images, image_coupling,
    own_rows, other_rows, split_rows, columns, order, place, gathered, own_low,
    partial, other_partial, coarse, amounts, projected, gram, sums, slots,
    load_sem, vector_sem, block_sem, row_sem, out_sem,
    halo_send, halo_recv, gather_send, gather_recv, row_send, row_recv,
    edge_send, edge_recv, column_send, column_recv,
    partial_send, partial_recv, sum_send, sum_recv,
):
    grp = lax.axis_index("grp")
    sub = lax.axis_index("sub")
    y, z, x, core = grp // SIDE, grp % SIDE, sub // 2, sub % 2
    me = grp * 8 + sub
    place_of = {"x": x, "y": y, "z": z}

    def along_chain(step):
        device = (me + step + DEVICES) % DEVICES
        return (device // 8, device % 8)

    before_id, after_id = along_chain(-1), along_chain(1)
    chip_before_id, chip_after_id = along_chain(-2), along_chain(2)
    core_id = (grp, x * 2 + 1 - core)

    def chip(at_x, at_y, at_z):
        return (at_y * SIDE + at_z, at_x * 2 + core)

    def partner(axis, step):
        spot = dict(place_of)
        spot[axis] = (spot[axis] + step) % SIDE
        return chip(spot["x"], spot["y"], spot["z"])

    z_low, z_high = z % 2, z // 2
    sum_groups = (
        (z_low * SIDE + x, [
            chip((x + step) % SIDE, y, 2 * z_high + (z_low + flip) % 2)
            for flip in (0, 1) for step in range(SIDE) if flip or step
        ]),
        (z_high * SIDE + y, [
            chip(x, (y + step) % SIDE, 2 * ((z_high + flip) % 2) + z_low)
            for flip in (0, 1) for step in range(SIDE) if flip or step
        ]),
    )

    def load_copy(plane):
        return pltpu.make_async_copy(loads_h.at[plane], v0.at[plane], load_sem.at[plane])

    def vector_copy(plane):
        return pltpu.make_async_copy(
            deflation_h.at[plane], padded_vectors.at[NDEF:2 * NDEF, lanes(plane + 1)],
            vector_sem.at[plane],
        )

    block_copies = [
        pltpu.make_async_copy(source, target, block_sem.at[i])
        for i, (source, target) in enumerate([
            (local_h.at[0], precond.at[:, 0]),
            (local_h.at[1], precond.at[:, 1]),
            (local_h.at[2], precond.at[:, 2]),
            (lower_h, coupling.at[:, 0]),
            (diagonal_h, coupling.at[:, 1]),
            (upper_h, coupling.at[:, 2]),
        ])
    ]
    row_copy = pltpu.make_async_copy(inverse_h, own_rows, row_sem.at[0])
    order_copy = pltpu.make_async_copy(order_h, order, row_sem.at[1])
    for plane in (0, 7, 1, 2, 3, 4, 5, 6):
        load_copy(plane).start()
    for plane in range(L):
        vector_copy(plane).start()
    row_copy.start()
    order_copy.start()

    barrier = pltpu.get_barrier_semaphore()
    partners = [partner(axis, step) for axis in "xyz" for step in (1, 2, 3)]
    partners += [core_id, before_id, after_id, chip_before_id, chip_after_id]
    partners += sum_groups[0][1] + sum_groups[1][1]
    for device in partners:
        pl.semaphore_signal(barrier, inc=1, device_id=device, device_id_type=MESH)

    padded_vectors[:NDEF] = jnp.zeros((NDEF, (L + 2) * W), BF16)
    padded_vectors[2 * NDEF:] = jnp.zeros((NDEF, (L + 2) * W), BF16)
    padded_vectors[NDEF:2 * NDEF, :W] = jnp.zeros((NDEF, W), BF16)
    padded_vectors[NDEF:2 * NDEF, (L + 1) * W:] = jnp.zeros((NDEF, W), BF16)
    expansion[...] = jnp.zeros((2 * 128, L * W), BF16)
    images[...] = jnp.zeros((3 * 128, L * W), BF16)
    own_low[...] = jnp.zeros((2, SIDE * NDEF, K), BF16)
    gram[...] = jnp.zeros((K, 128), F32)
    projected[...] = jnp.zeros((NDEF, K), F32)
    coarse[...] = jnp.zeros((128, K), F32)

    pl.semaphore_wait(barrier, len(partners))

    sends = []

    def remote(source, target, send, recv, device):
        return pltpu.make_async_remote_copy(
            src_ref=source, dst_ref=target, send_sem=send, recv_sem=recv,
            device_id=device, device_id_type=MESH,
        )

    def start(copies):
        for copy in copies:
            copy.start()
        sends.extend(copies)

    def received(copies):
        for copy in copies:
            copy.wait_recv()

    row_exchange = [
        remote(inverse_h, other_rows, row_send.at[0], row_recv.at[0], core_id)
    ]
    edge_exchange = [
        remote(
            deflation_h.at[0], edge_vectors.at[1], edge_send.at[0], edge_recv.at[0], before_id
        ),
        remote(
            deflation_h.at[L - 1], edge_vectors.at[0], edge_send.at[1], edge_recv.at[1], after_id
        ),
    ]
    column_exchange = [
        remote(
            columns.at[row:row + NDEF], columns.at[target:target + NDEF],
            column_send.at[i], column_recv.at[i], device,
        )
        for i, (row, target, device) in enumerate([
            (2 * NDEF, 0, chip_after_id),
            (6 * NDEF, 4 * NDEF, chip_after_id),
            (NDEF, 3 * NDEF, chip_before_id),
            (5 * NDEF, 7 * NDEF, chip_before_id),
        ])
    ]

    def halo_copies(field, which):
        return [
            remote(
                field.at[:, lanes(1)], field.at[:, lanes(L + 1)],
                halo_send.at[which, 0], halo_recv.at[which, 0], before_id,
            ),
            remote(
                field.at[:, lanes(L)], field.at[:, lanes(0)],
                halo_send.at[which, 1], halo_recv.at[which, 1], after_id,
            ),
        ]

    def start_halo(field, which):
        start(halo_copies(field, which))

    def finish_halo(field, which):
        received(halo_copies(field, which))

        @pl.when(me == 0)
        def _():
            field[:, lanes(0)] = jnp.zeros((K, W), BF16)

        @pl.when(me == DEVICES - 1)
        def _():
            field[:, lanes(L + 1)] = jnp.zeros((K, W), BF16)

    def gather_copies(which, stage):
        found = []
        for part, (axes, row0, row1, lane0, lane1) in enumerate(GATHER_PARTS):
            done = axes[:stage]
            spot = tuple(slice(None) if name in done else place_of[name] for name in "yzx")
            block = gathered.at[(which,) + spot + (slice(row0, row1), slice(lane0, lane1))]
            for step in (1, 2, 3):
                found.append(remote(
                    block, block,
                    gather_send.at[which, part, stage, step - 1],
                    gather_recv.at[which, part, stage, step - 1],
                    partner(axes[stage], step),
                ))
        return found

    def start_gather(which, stage):
        start(gather_copies(which, stage))

    def finish_gather(which, stage):
        received(gather_copies(which, stage))

    def share_coefficients(own, which):
        high, low = two_terms(own)
        gathered[which, y, z, x] = high
        start_gather(which, 0)
        own_low[which, pl.ds(pl.multiple_of(x * NDEF, NDEF), NDEF)] = low

    def banded(field, blocks, plane):
        window = field[:, pl.ds(pl.multiple_of(plane * W, W), BAND)]
        return dot(window, blocks[plane].reshape(BAND, W))

    def edge(i):
        return i * (L - 1)

    def finish_coarse(which):
        product = dot(columns[...], gathered[which].reshape(SAME, K))
        window = pl.ds(pl.multiple_of((y * SIDE + z) * 128, 128), 128)
        fix = dot(columns[:4 * NDEF, window], own_low[which])
        partial[which] = product[:4 * NDEF] + (product[4 * NDEF:] + fix)
        exchange = [remote(
            partial.at[which, pl.ds(pl.multiple_of((1 - core) * NDEF, NDEF), 3 * NDEF)],
            other_partial.at[which], partial_send.at[which], partial_recv.at[which], core_id,
        )]
        start(exchange)
        received(exchange)
        coarse[:3 * NDEF] = (
            partial[which, pl.ds(pl.multiple_of(core * NDEF, NDEF), 3 * NDEF)]
            + other_partial[which]
        )
        high, low = two_terms(jnp.transpose(coarse[...]))
        amounts[which, :, :128] = high
        amounts[which, :, 128:256] = low
        amounts[which, :, 256:] = high

    def precondition(field, result, rounded, which):
        def apply(plane):
            value = banded(field, precond, plane)
            result[plane] = value
            rounded[:, lanes(plane + 1)] = value.astype(BF16)

        finish_halo(field, 2 * which)

        @pl.loop(0, 2)
        def _(i):
            apply(edge(i))

        start_halo(rounded, 2 * which + 1)

        @pl.loop(1, L - 1)
        def _(plane):
            apply(plane)

    def operate(field, result, which, planes, project):
        @pl.loop(*planes)
        def _(i):
            plane = i if planes == (1, L - 1) else edge(i)
            image = banded(field, coupling, plane)
            result[plane] = image
            if project:
                projected[...] += dot(
                    padded_vectors[NDEF:2 * NDEF, lanes(plane + 1)], image.astype(BF16), NT
                )

    def add_image(result, rounded, plane, which):
        total = result[plane] + dot(amounts[which], images[:, lanes(plane)])
        result[plane] = total
        if rounded is not None:
            rounded[:, lanes(plane + 1)] = total.astype(BF16)

    def add_expansion(result, which):
        @pl.loop(0, L)
        def _(plane):
            result[plane] += dot(amounts[which, :, :256], expansion[:, lanes(plane)])

    def inner_products(pairs):
        rows = 32

        @pl.loop(0, K // rows)
        def _(chunk):
            span = pl.ds(pl.multiple_of(chunk * rows, rows), rows)
            for column, first, second in pairs:
                total = jnp.zeros((rows, 128), F32)
                for plane in range(L):
                    for lane in range(0, W, 128):
                        one = first[plane, span, lane:lane + 128]
                        two = second[plane, span, lane:lane + 128]
                        if first is u1:
                            one = one * IMAGE_SCALE
                        if second is u1:
                            two = two * IMAGE_SCALE
                        total += one * two
                gram[span, column:column + 1] = jnp.sum(total, axis=1, keepdims=True)

    def permute_columns(first, last):
        @pl.loop(first, last)
        def _(block):
            base = block * 256
            total = jnp.zeros((4 * NDEF, 256), F32)
            for part in range(4):
                span = slice(part * 1024, (part + 1) * 1024)
                row = lax.broadcasted_iota(jnp.int32, (256, 1024), 0)
                hot = jnp.where(place[:, span] - base == row, 1.0, 0.0).astype(BF16)
                total += dot(split_rows[:, span], hot, NT)
            target = pl.ds(pl.multiple_of(base, 256), 256)
            columns[NDEF:3 * NDEF, target] = total[:2 * NDEF].astype(BF16)
            columns[5 * NDEF:7 * NDEF, target] = total[2 * NDEF:].astype(BF16)

    start(row_exchange)
    start(edge_exchange)

    def round_load(plane):
        load_copy(plane).wait()
        field0[:, lanes(plane + 1)] = v0[plane].astype(BF16)

    round_load(0)
    round_load(L - 1)
    start_halo(field0, 0)

    @pl.loop(1, L - 1)
    def _(plane):
        round_load(plane)

    @pl.loop(0, L)
    def _(plane):
        vector_copy(plane).wait()

    for copy in block_copies:
        copy.start()

    share_coefficients(
        dot(padded_vectors[NDEF:2 * NDEF, W:(L + 1) * W], field0[:, W:(L + 1) * W], NT), 0
    )

    row_copy.wait()
    order_copy.wait()
    received(row_exchange)
    for rows, owner in ((own_rows, core), (other_rows, 1 - core)):
        high, low = two_terms(rows[...])
        split_rows[pl.ds(pl.multiple_of(owner * NDEF, NDEF), NDEF)] = high
        split_rows[pl.ds(pl.multiple_of((2 + owner) * NDEF, NDEF), NDEF)] = low
    unknown = order[...]
    inside = unknown % (2 * NDEF)
    place[...] = jnp.where(
        inside // NDEF == core, unknown // (2 * NDEF) * NDEF + inside % NDEF, -1
    )
    permute_columns(0, 3)
    finish_gather(0, 0)
    start_gather(0, 1)
    permute_columns(3, SAME // 256)
    start(column_exchange)
    finish_gather(0, 1)
    start_gather(0, 2)

    for copy in block_copies[:3]:
        copy.wait()
    precondition(field0, z0, field1, 0)
    for copy in block_copies[3:]:
        copy.wait()
    operate(field1, u0, 0, (1, L - 1), True)
    received(edge_exchange)
    padded_vectors[:NDEF, :W] = jnp.where(me > 0, edge_vectors[0], 0)
    padded_vectors[2 * NDEF:, (L + 1) * W:] = jnp.where(me < DEVICES - 1, edge_vectors[1], 0)

    @pl.loop(0, L)
    def _(plane):
        high, low = two_terms(banded(padded_vectors, coupling, plane))
        images[:3 * NDEF, lanes(plane)] = high
        images[128:128 + 3 * NDEF, lanes(plane)] = high
        images[256:256 + 3 * NDEF, lanes(plane)] = low
        own = padded_vectors[NDEF:2 * NDEF, lanes(plane + 1)]
        expansion[NDEF:2 * NDEF, lanes(plane)] = own
        expansion[128 + NDEF:128 + 2 * NDEF, lanes(plane)] = own

    vectors = padded_vectors[NDEF:2 * NDEF, W:(L + 1) * W]
    image_coupling[...] = dot(vectors, images[:128], NT) + dot(vectors, images[256:], NT)
    finish_halo(field1, 1)
    operate(field1, u0, 0, (0, 2), True)
    finish_gather(0, 2)
    received(column_exchange)
    finish_coarse(0)
    share_coefficients(
        projected[...] + dot(image_coupling[...], coarse[...], NN, lax.Precision.HIGHEST), 1
    )

    @pl.loop(0, 2)
    def _(i):
        add_image(u0, field2, edge(i), 0)

    start_halo(field2, 2)

    @pl.loop(1, L - 1)
    def _(plane):
        add_image(u0, field2, plane, 0)

    finish_gather(1, 0)
    start_gather(1, 1)
    inner_products(((0, v0, v0), (1, v0, u0), (2, u0, u0)))
    precondition(field2, z1, field3, 1)
    finish_gather(1, 1)
    start_gather(1, 2)
    operate(field3, u1, 1, (1, L - 1), False)
    finish_halo(field3, 3)
    operate(field3, u1, 1, (0, 2), False)
    add_expansion(z0, 0)
    finish_gather(1, 2)
    finish_coarse(1)

    @pl.loop(0, L)
    def _(plane):
        add_image(u1, None, plane, 1)

    inner_products(((3, v0, u1), (4, u0, u1), (5, u1, u1)))
    sums[...] = jnp.transpose(gram[...])[:8]

    pair = remote(sums, slots.at[0, 0], sum_send.at[0, 0], sum_recv.at[0, 0], core_id)
    pair.start()
    pair.wait()
    sums[...] = sums[...] + slots[0, 0]
    for stage, (spot, group) in enumerate(sum_groups):
        slots[1 + stage, spot] = sums[...]
        copies = [
            remote(
                slots.at[1 + stage, spot], slots.at[1 + stage, spot],
                sum_send.at[1 + stage, i], sum_recv.at[1 + stage, i], device,
            )
            for i, device in enumerate(group)
        ]
        for copy in copies:
            copy.start()
        if stage == 0:
            add_expansion(z1, 1)
        for copy in copies:
            copy.wait()
        sums[...] = (
            ((slots[1 + stage, 0] + slots[1 + stage, 1])
             + (slots[1 + stage, 2] + slots[1 + stage, 3]))
            + ((slots[1 + stage, 4] + slots[1 + stage, 5])
               + (slots[1 + stage, 6] + slots[1 + stage, 7]))
        )

    g00, g01, g11 = sums[0:1], sums[1:2], sums[2:3]
    g02, g12, g22 = sums[3:4], sums[4:5], sums[5:6]
    s0, s1, s2 = jnp.sqrt(g00), jnp.sqrt(g11), jnp.sqrt(g22)
    r01 = g01 / s0 / s1
    r02 = g02 / s0 / s2
    r11 = jnp.sqrt((1.0 - r01) * (1.0 + r01))
    r12 = (g12 / s1 / s2 - r01 * r02) / r11
    r22 = jnp.sqrt((1.0 - r02) * (1.0 + r02) - r12 * r12)
    n0 = r11 * r22
    n1 = r01 * r22
    n2 = r01 * r12 - r11 * r02
    share = n0 / (n0 * n0 + n1 * n1 + n2 * n2)
    relative_ref[...] = n0 * share
    scaled1 = -(share * n2) / r22
    weight1 = scaled1 * (s0 / s2) * IMAGE_SCALE
    weight0 = (share * n1 - scaled1 * r12) / r11 * (s0 / s1)
    gram[...] = jnp.transpose(
        jnp.concatenate([weight0, weight1, jnp.zeros((126, K), F32)], axis=0)
    )

    def solution_copy(plane):
        return pltpu.make_async_copy(z0.at[plane], solution_h.at[plane], out_sem.at[0, plane])

    def residual_copy(plane):
        return pltpu.make_async_copy(v0.at[plane], residual_h.at[plane], out_sem.at[1, plane])

    @pl.loop(0, L)
    def _(plane):
        first = gram[:, 0:1]
        second = gram[:, 1:2]
        z0[plane] = first * z0[plane] + second * z1[plane]
        solution_copy(plane).start()
        v0[plane] = v0[plane] - first * u0[plane] - second * u1[plane]
        residual_copy(plane).start()

    for copy in sends:
        copy.wait_send()

    @pl.loop(0, L)
    def _(plane):
        solution_copy(plane).wait()
        residual_copy(plane).wait()


def local(
    loads, diagonal_blocks, lower_coupling, upper_coupling, local_inverse, deflation,
    coarse_inverse, coarse_order,
):
    hbm = pl.BlockSpec(memory_space=pl.ANY)
    field = pltpu.VMEM((L, K, W), F32)
    padded = pltpu.VMEM((K, (L + 2) * W), BF16)
    blocks = pltpu.VMEM((L, 3, W, W), BF16)
    dma = pltpu.SemaphoreType.DMA
    answer, residual, relative = pl.pallas_call(
        kernel,
        out_shape=(
            jax.ShapeDtypeStruct((L, K, W), F32),
            jax.ShapeDtypeStruct((L, K, W), F32),
            jax.ShapeDtypeStruct((1, K), F32),
        ),
        in_specs=[hbm] * 8,
        out_specs=(hbm, hbm, pl.BlockSpec(memory_space=pltpu.VMEM)),
        scratch_shapes=[
            field, field, field, field, field,
            padded, padded, padded, padded,
            blocks, blocks,
            pltpu.VMEM((3 * NDEF, (L + 2) * W), BF16),
            pltpu.VMEM((2, NDEF, W), BF16),
            pltpu.VMEM((2 * 128, L * W), BF16),
            pltpu.VMEM((3 * 128, L * W), BF16),
            pltpu.VMEM((NDEF, 128), F32),
            pltpu.VMEM((NDEF, NCOARSE), F32),
            pltpu.VMEM((NDEF, NCOARSE), F32),
            pltpu.VMEM((4 * NDEF, NCOARSE), BF16),
            pltpu.VMEM((8 * NDEF, SAME), BF16),
            pltpu.VMEM((1, NCOARSE), jnp.int32),
            pltpu.VMEM((1, NCOARSE), jnp.int32),
            pltpu.VMEM((2, SIDE, SIDE, SIDE, NDEF, K), BF16),
            pltpu.VMEM((2, SIDE * NDEF, K), BF16),
            pltpu.VMEM((2, 4 * NDEF, K), F32),
            pltpu.VMEM((2, 3 * NDEF, K), F32),
            pltpu.VMEM((128, K), F32),
            pltpu.VMEM((2, K, 3 * 128), BF16),
            pltpu.VMEM((NDEF, K), F32),
            pltpu.VMEM((K, 128), F32),
            pltpu.VMEM((8, K), F32),
            pltpu.VMEM((3, 8, 8, K), F32),
            dma((L,)), dma((L,)), dma((6,)), dma((2,)), dma((2, L)),
            dma((4, 2)), dma((4, 2)), dma((2, 3, 3, 3)), dma((2, 3, 3, 3)),
            dma((1,)), dma((1,)), dma((2,)), dma((2,)), dma((4,)), dma((4,)),
            dma((2,)), dma((2,)), dma((3, 7)), dma((3, 7)),
        ],
        compiler_params=pltpu.CompilerParams(
            collective_id=0, has_side_effects=True, vmem_limit_bytes=60 * 2**20
        ),
        cost_estimate=pl.CostEstimate(
            flops=8 * 10**9, bytes_accessed=25 * 10**6, transcendentals=0
        ),
    )(
        loads, diagonal_blocks, lower_coupling, upper_coupling, local_inverse, deflation,
        coarse_inverse, coarse_order.reshape(1, NCOARSE),
    )
    return answer, residual, relative.reshape(K)


def solution(mesh):
    spread = P(("grp", "sub"))
    return jax.shard_map(
        local,
        mesh=mesh,
        in_specs=(
            spread, spread, spread, spread, P(None, ("grp", "sub")), spread, spread, P(),
        ),
        out_specs=(spread, spread, P()),
        check_vma=False,
    )
```

time: 87.6 us -> 83.4 us (0.952)
  Pallas kernels: 80.7 us -> 76.5 us
    pallas_call x1, Pallas kernels: 80.7 us -> 76.5 us  [local(): pl.pallas_call(kernel, out_shape=(jax.ShapeDtypeStruct((L, K, W), F32), j...]
where the time goes in v2:
time: 83.4 us; the launch traced here: 83.3 us
  Pallas kernels  76.5 us (92%)
  local copies, waits for them, and re-layouts  6.17 us (7%)
    pallas_call x1, Pallas kernels, local(): pl.pallas_call(kernel, out_shape=(jax.ShapeDtypeStruct((L, K, W), F32), j...  76.5 us
    unnamed x7, local copies, waits for them, and re-layouts  6.17 us

profile of v2, /device:TPU:0, one launch (start us, length us, event | category | flops | bytes accessed | tf_op | source)
XLA Modules:
  0.0 83.3 jit_solution(17849052145549665913)
XLA Ops:
  0.6 76.5 %shard_map.103 = (f32[8,256,384]{2,1,0:T(8,128)}, f32[8,256,384]{2,1,0:T(8,128)}, f32[1,256]{1,0:T(1,128)}) custom-call(f32[8,256,384]{2,1,0:T(8,128)} %loads_h.1, bf16[8,384,384]{2,1,0:T(8,128)(2,1)} %diagonal_h.1, bf16[8,384,384]{2,1,0:T(8,128)(2,1)} %lower_h.1, bf16[8,384,384]{2,1,0:T(8,128)(2,1)} %upper_h.1, bf16[3,8,384,384]{3,2,1,0:T(8,128)(2,1)} %local_h.1, ...), custom_call_target="tpu_custom_call" | custom-call | flops 8000000000 | bytes 25000000 | tf_op jit(solution)/shard_map/pallas_call | solution.py:521
  77.1 0.0 copy-start
  77.1 3.9 %copy.14 = f32[8,256,384]{2,1,0:T(8,128)} copy(f32[8,256,384]{2,1,0:T(8,128)} %get-tuple-element.12) | data formatting | bytes 6291456
  81.0 0.0 copy-done
  81.0 0.0 copy-start.1
  81.0 1.7 %copy.15 = f32[8,256,384]{2,1,0:T(8,128)} copy(f32[8,256,384]{2,1,0:T(8,128)S(1)} %copy-done) | data formatting | bytes 6291456
  82.7 0.0 copy-done.1
  82.7 0.6 copy.16
Async XLA Ops:
  77.1 3.9 %copy-start = (f32[8,256,384]{2,1,0:T(8,128)S(1)}, f32[8,256,384]{2,1,0:T(8,128)}, u32[]{:S(2)}) copy-start(f32[8,256,384]{2,1,0:T(8,128)} %get-tuple-element.13) | copy-start | bytes 9437188
  81.0 1.7 %copy-start.1 = (f32[1,256]{1,0:T(1,128)S(1)}, f32[1,256]{1,0:T(1,128)}, u32[]{:S(2)}) copy-start(f32[1,256]{1,0:T(1,128)} %get-tuple-element.8) | copy-start | bytes 3076

commit v3 on v2

--- a/solution.py
+++ b/solution.py
@@ -19,11 +19,8 @@
 NCOARSE = 2 * SAME
 BAND = 3 * W
 IMAGE_SCALE = 2.0 ** -24
-GATHER_PARTS = (
-    ("xyz", 0, 16, 0, 256),
-    ("yzx", 16, 32, 0, 128),
-    ("zxy", 16, 32, 128, 256),
-)
+INNER, OUTER = (1, L - 1), (0, 2)
+GATHER_PARTS = (("xyz", 0, 16), ("zxy", 16, 32))
 NN = (((1,), (0,)), ((), ()))
 NT = (((1,), (1,)), ((), ()))
 
@@ -119,9 +116,9 @@
     order_copy.start()
 
     barrier = pltpu.get_barrier_semaphore()
+    outer = (me + DEVICES - 1 + 2 * core) % DEVICES
     partners = [partner(axis, step) for axis in "xyz" for step in (1, 2, 3)]
-    partners += [core_id, before_id, after_id, chip_before_id, chip_after_id]
-    partners += sum_groups[0][1] + sum_groups[1][1]
+    partners += [core_id, (outer // 8, outer % 8), chip_before_id, chip_after_id]
     for device in partners:
         pl.semaphore_signal(barrier, inc=1, device_id=device, device_id_type=MESH)
 
@@ -135,8 +132,6 @@
     gram[...] = jnp.zeros((K, 128), F32)
     projected[...] = jnp.zeros((NDEF, K), F32)
     coarse[...] = jnp.zeros((128, K), F32)
-
-    pl.semaphore_wait(barrier, len(partners))
 
     sends = []
 
@@ -207,10 +202,10 @@
 
     def gather_copies(which, stage):
         found = []
-        for part, (axes, row0, row1, lane0, lane1) in enumerate(GATHER_PARTS):
+        for part, (axes, row0, row1) in enumerate(GATHER_PARTS):
             done = axes[:stage]
             spot = tuple(slice(None) if name in done else place_of[name] for name in "yzx")
-            block = gathered.at[(which,) + spot + (slice(row0, row1), slice(lane0, lane1))]
+            block = gathered.at[(which,) + spot + (slice(row0, row1),)]
             for step in (1, 2, 3):
                 found.append(remote(
                     block, block,
@@ -259,28 +254,18 @@
         amounts[which, :, 128:256] = low
         amounts[which, :, 256:] = high
 
-    def precondition(field, result, rounded, which):
-        def apply(plane):
+    def precondition(field, result, rounded, planes):
+        @pl.loop(*planes)
+        def _(i):
+            plane = i if planes == INNER else edge(i)
             value = banded(field, precond, plane)
             result[plane] = value
             rounded[:, lanes(plane + 1)] = value.astype(BF16)
 
-        finish_halo(field, 2 * which)
-
-        @pl.loop(0, 2)
-        def _(i):
-            apply(edge(i))
-
-        start_halo(rounded, 2 * which + 1)
-
-        @pl.loop(1, L - 1)
-        def _(plane):
-            apply(plane)
-
-    def operate(field, result, which, planes, project):
+    def operate(field, result, planes, project):
         @pl.loop(*planes)
         def _(i):
-            plane = i if planes == (1, L - 1) else edge(i)
+            plane = i if planes == INNER else edge(i)
             image = banded(field, coupling, plane)
             result[plane] = image
             if project:
@@ -299,23 +284,23 @@
         def _(plane):
             result[plane] += dot(amounts[which, :, :256], expansion[:, lanes(plane)])
 
-    def inner_products(pairs):
+    def inner_products(fields, pairs):
         rows = 32
 
         @pl.loop(0, K // rows)
         def _(chunk):
             span = pl.ds(pl.multiple_of(chunk * rows, rows), rows)
-            for column, first, second in pairs:
-                total = jnp.zeros((rows, 128), F32)
-                for plane in range(L):
-                    for lane in range(0, W, 128):
-                        one = first[plane, span, lane:lane + 128]
-                        two = second[plane, span, lane:lane + 128]
-                        if first is u1:
-                            one = one * IMAGE_SCALE
-                        if second is u1:
-                            two = two * IMAGE_SCALE
-                        total += one * two
+            totals = [jnp.zeros((rows, 128), F32) for _ in pairs]
+            for plane in range(L):
+                for lane in range(0, W, 128):
+                    values = [field[plane, span, lane:lane + 128] for field in fields]
+                    if len(values) == 3:
+                        values[2] = values[2] * IMAGE_SCALE
+                    totals = [
+                        total + values[first] * values[second]
+                        for total, (_, first, second) in zip(totals, pairs)
+                    ]
+            for total, (column, _, _) in zip(totals, pairs):
                 gram[span, column:column + 1] = jnp.sum(total, axis=1, keepdims=True)
 
     def permute_columns(first, last):
@@ -332,31 +317,22 @@
             columns[NDEF:3 * NDEF, target] = total[:2 * NDEF].astype(BF16)
             columns[5 * NDEF:7 * NDEF, target] = total[2 * NDEF:].astype(BF16)
 
-    start(row_exchange)
-    start(edge_exchange)
-
-    def round_load(plane):
+    for plane in (0, 7, 1, 2, 3, 4, 5, 6):
         load_copy(plane).wait()
         field0[:, lanes(plane + 1)] = v0[plane].astype(BF16)
 
-    round_load(0)
-    round_load(L - 1)
-    start_halo(field0, 0)
-
-    @pl.loop(1, L - 1)
-    def _(plane):
-        round_load(plane)
-
-    @pl.loop(0, L)
-    def _(plane):
+    for plane in range(L):
         vector_copy(plane).wait()
-
     for copy in block_copies:
         copy.start()
-
-    share_coefficients(
-        dot(padded_vectors[NDEF:2 * NDEF, W:(L + 1) * W], field0[:, W:(L + 1) * W], NT), 0
-    )
+    first_coefficients = dot(
+        padded_vectors[NDEF:2 * NDEF, W:(L + 1) * W], field0[:, W:(L + 1) * W], NT
+    )
+    pl.semaphore_wait(barrier, len(partners))
+    share_coefficients(first_coefficients, 0)
+    start(row_exchange)
+    start_halo(field0, 0)
+    start(edge_exchange)
 
     row_copy.wait()
     order_copy.wait()
@@ -380,10 +356,13 @@
 
     for copy in block_copies[:3]:
         copy.wait()
-    precondition(field0, z0, field1, 0)
+    finish_halo(field0, 0)
+    precondition(field0, z0, field1, OUTER)
+    start_halo(field1, 1)
+    precondition(field0, z0, field1, INNER)
     for copy in block_copies[3:]:
         copy.wait()
-    operate(field1, u0, 0, (1, L - 1), True)
+    operate(field1, u0, INNER, True)
     received(edge_exchange)
     padded_vectors[:NDEF, :W] = jnp.where(me > 0, edge_vectors[0], 0)
     padded_vectors[2 * NDEF:, (L + 1) * W:] = jnp.where(me < DEVICES - 1, edge_vectors[1], 0)
@@ -401,7 +380,7 @@
     vectors = padded_vectors[NDEF:2 * NDEF, W:(L + 1) * W]
     image_coupling[...] = dot(vectors, images[:128], NT) + dot(vectors, images[256:], NT)
     finish_halo(field1, 1)
-    operate(field1, u0, 0, (0, 2), True)
+    operate(field1, u0, OUTER, True)
     finish_gather(0, 2)
     received(column_exchange)
     finish_coarse(0)
@@ -421,14 +400,17 @@
 
     finish_gather(1, 0)
     start_gather(1, 1)
-    inner_products(((0, v0, v0), (1, v0, u0), (2, u0, u0)))
-    precondition(field2, z1, field3, 1)
+    inner_products((v0, u0), ((0, 0, 0), (1, 0, 1), (2, 1, 1)))
+    precondition(field2, z1, field3, INNER)
     finish_gather(1, 1)
     start_gather(1, 2)
-    operate(field3, u1, 1, (1, L - 1), False)
+    finish_halo(field2, 2)
+    precondition(field2, z1, field3, OUTER)
+    start_halo(field3, 3)
+    operate(field3, u1, INNER, False)
+    add_expansion(z0, 0)
     finish_halo(field3, 3)
-    operate(field3, u1, 1, (0, 2), False)
-    add_expansion(z0, 0)
+    operate(field3, u1, OUTER, False)
     finish_gather(1, 2)
     finish_coarse(1)
 
@@ -436,7 +418,7 @@
     def _(plane):
         add_image(u1, None, plane, 1)
 
-    inner_products(((3, v0, u1), (4, u0, u1), (5, u1, u1)))
+    inner_products((v0, u0, u1), ((3, 0, 2), (4, 1, 2), (5, 2, 2)))
     sums[...] = jnp.transpose(gram[...])[:8]
 
     pair = remote(sums, slots.at[0, 0], sum_send.at[0, 0], sum_recv.at[0, 0], core_id)
@@ -493,8 +475,7 @@
 
     @pl.loop(0, L)
     def _(plane):
-        first = gram[:, 0:1]
-        second = gram[:, 1:2]
+        first, second = gram[:, 0:1], gram[:, 1:2]
         z0[plane] = first * z0[plane] + second * z1[plane]
         solution_copy(plane).start()
         v0[plane] = v0[plane] - first * u0[plane] - second * u1[plane]
@@ -507,6 +488,30 @@
     def _(plane):
         solution_copy(plane).wait()
         residual_copy(plane).wait()
+
+
+def deliver(
+    answer, residual, relative, answer_out, residual_out, relative_out, held, held_row, sems
+):
+    def through(source, between, target, i, j):
+        return (
+            pltpu.make_async_copy(source, between, sems.at[0, i, j]),
+            pltpu.make_async_copy(between, target, sems.at[1, i, j]),
+        )
+
+    steps = [
+        through(source.at[plane], held.at[i, plane], target.at[plane], i, plane)
+        for plane in range(L)
+        for i, (source, target) in enumerate(((answer, answer_out), (residual, residual_out)))
+    ]
+    steps.append(through(relative, held_row, relative_out, 2, 0))
+    for fetch, _ in steps:
+        fetch.start()
+    for fetch, store in steps:
+        fetch.wait()
+        store.start()
+    for _, store in steps:
+        store.wait()
 
 
 def local(
@@ -518,13 +523,11 @@
     padded = pltpu.VMEM((K, (L + 2) * W), BF16)
     blocks = pltpu.VMEM((L, 3, W, W), BF16)
     dma = pltpu.SemaphoreType.DMA
-    answer, residual, relative = pl.pallas_call(
+    fields = jax.ShapeDtypeStruct((L, K, W), F32)
+    outs = (fields, fields, jax.ShapeDtypeStruct((1, K), F32))
+    results = pl.pallas_call(
         kernel,
-        out_shape=(
-            jax.ShapeDtypeStruct((L, K, W), F32),
-            jax.ShapeDtypeStruct((L, K, W), F32),
-            jax.ShapeDtypeStruct((1, K), F32),
-        ),
+        out_shape=outs,
         in_specs=[hbm] * 8,
         out_specs=(hbm, hbm, pl.BlockSpec(memory_space=pltpu.VMEM)),
         scratch_shapes=[
@@ -553,7 +556,7 @@
             pltpu.VMEM((8, K), F32),
             pltpu.VMEM((3, 8, 8, K), F32),
             dma((L,)), dma((L,)), dma((6,)), dma((2,)), dma((2, L)),
-            dma((4, 2)), dma((4, 2)), dma((2, 3, 3, 3)), dma((2, 3, 3, 3)),
+            dma((4, 2)), dma((4, 2)), dma((2, 2, 3, 3)), dma((2, 2, 3, 3)),
             dma((1,)), dma((1,)), dma((2,)), dma((2,)), dma((4,)), dma((4,)),
             dma((2,)), dma((2,)), dma((3, 7)), dma((3, 7)),
         ],
@@ -567,7 +570,15 @@
         loads, diagonal_blocks, lower_coupling, upper_coupling, local_inverse, deflation,
         coarse_inverse, coarse_order.reshape(1, NCOARSE),
     )
-    return answer, residual, relative.reshape(K)
+    answer, residual, ratio = pl.pallas_call(
+        deliver,
+        out_shape=outs,
+        in_specs=[hbm] * 3,
+        out_specs=(hbm,) * 3,
+        scratch_shapes=[pltpu.VMEM((2, L, K, W), F32), pltpu.VMEM((1, K), F32), dma((2, 3, L))],
+        compiler_params=pltpu.CompilerParams(vmem_limit_bytes=60 * 2**20),
+    )(*results)
+    return answer, residual, ratio.reshape(K)
 
 
 def solution(mesh):

time: 83.4 us -> 79.4 us (0.952)
  local copies, waits for them, and re-layouts: 6.17 us -> 0 us
  Pallas kernels: 76.5 us -> 78.7 us
    unnamed x7 -> x0, local copies, waits for them, and re-layouts: 6.17 us -> none
    pallas_call x1 -> x2, Pallas kernels: 76.5 us -> 78.7 us  [the longest x1 73 us: local(): pl.pallas_call(kernel, out_shape=outs, in_specs=[hbm] * 8, out_specs=(hbm...]
where the time goes in v3:
time: 79.4 us; the launch traced here: 79.3 us
  Pallas kernels  78.7 us (99%)
    pallas_call x1, Pallas kernels, local(): pl.pallas_call(kernel, out_shape=outs, in_specs=[hbm] * 8, out_specs=(hbm...  73 us
    pallas_call x1, Pallas kernels, local(): pl.pallas_call(deliver, out_shape=outs, in_specs=[hbm] * 3, out_specs=(hb...  5.63 us

profile of v3, /device:TPU:0, one launch (start us, length us, event | category | flops | bytes accessed | tf_op | source)
XLA Modules:
  0.0 79.3 jit_solution(18373826283641378691)
XLA Ops:
  0.6 73.0 %shard_map.103 = (f32[8,256,384]{2,1,0:T(8,128)}, f32[8,256,384]{2,1,0:T(8,128)}, f32[1,256]{1,0:T(1,128)}) custom-call(f32[8,256,384]{2,1,0:T(8,128)} %loads_h.1, bf16[8,384,384]{2,1,0:T(8,128)(2,1)} %diagonal_h.1, bf16[8,384,384]{2,1,0:T(8,128)(2,1)} %lower_h.1, bf16[8,384,384]{2,1,0:T(8,128)(2,1)} %upper_h.1, bf16[3,8,384,384]{3,2,1,0:T(8,128)(2,1)} %local_h.1, ...), custom_call_target="tpu_custom_call" | custom-call | flops 8000000000 | bytes 25000000 | tf_op jit(solution)/shard_map/pallas_call | solution.py:528
  73.7 5.6 %shard_map.104 = (f32[8,256,384]{2,1,0:T(8,128)}, f32[8,256,384]{2,1,0:T(8,128)}, f32[1,256]{1,0:T(1,128)}) custom-call(f32[8,256,384]{2,1,0:T(8,128)} %get-tuple-element.9.answer, f32[8,256,384]{2,1,0:T(8,128)} %get-tuple-element.10.residual, f32[1,256]{1,0:T(1,128)} %get-tuple-element.11.relative), custom_call_target="tpu_custom_call" | custom-call | tf_op jit(solution)/shard_map/pallas_call | solution.py:573

commit v4 on v3

--- a/solution.py
+++ b/solution.py
@@ -128,6 +128,8 @@
     padded_vectors[NDEF:2 * NDEF, (L + 1) * W:] = jnp.zeros((NDEF, W), BF16)
     expansion[...] = jnp.zeros((2 * 128, L * W), BF16)
     images[...] = jnp.zeros((3 * 128, L * W), BF16)
+    columns[4 * NDEF:5 * NDEF] = jnp.zeros((NDEF, SAME), BF16)
+    columns[7 * NDEF:] = jnp.zeros((NDEF, SAME), BF16)
     own_low[...] = jnp.zeros((2, SIDE * NDEF, K), BF16)
     gram[...] = jnp.zeros((K, 128), F32)
     projected[...] = jnp.zeros((NDEF, K), F32)
@@ -168,9 +170,7 @@
         )
         for i, (row, target, device) in enumerate([
             (2 * NDEF, 0, chip_after_id),
-            (6 * NDEF, 4 * NDEF, chip_after_id),
             (NDEF, 3 * NDEF, chip_before_id),
-            (5 * NDEF, 7 * NDEF, chip_before_id),
         ])
     ]
 
@@ -307,15 +307,19 @@
         @pl.loop(first, last)
         def _(block):
             base = block * 256
-            total = jnp.zeros((4 * NDEF, 256), F32)
+            total = jnp.zeros((256, 4 * NDEF), F32)
             for part in range(4):
                 span = slice(part * 1024, (part + 1) * 1024)
-                row = lax.broadcasted_iota(jnp.int32, (256, 1024), 0)
-                hot = jnp.where(place[:, span] - base == row, 1.0, 0.0).astype(BF16)
-                total += dot(split_rows[:, span], hot, NT)
+                spot = place[:, span] - base
+                inside = (spot >= 0) & (spot < 256)
+                spot = jnp.where(inside, spot, -1).astype(F32).astype(BF16)
+                row = lax.broadcasted_iota(jnp.int32, (256, 1024), 0).astype(F32).astype(BF16)
+                hot = jnp.where(spot == row, jnp.ones((), BF16), jnp.zeros((), BF16))
+                total += dot(hot, split_rows[:, span], NT)
+            total = jnp.transpose(total).astype(BF16)
             target = pl.ds(pl.multiple_of(base, 256), 256)
-            columns[NDEF:3 * NDEF, target] = total[:2 * NDEF].astype(BF16)
-            columns[5 * NDEF:7 * NDEF, target] = total[2 * NDEF:].astype(BF16)
+            columns[NDEF:3 * NDEF, target] = total[:2 * NDEF]
+            columns[5 * NDEF:7 * NDEF, target] = total[2 * NDEF:]
 
     for plane in (0, 7, 1, 2, 3, 4, 5, 6):
         load_copy(plane).wait()
@@ -346,13 +350,13 @@
     place[...] = jnp.where(
         inside // NDEF == core, unknown // (2 * NDEF) * NDEF + inside % NDEF, -1
     )
-    permute_columns(0, 3)
+    permute_columns(0, 4)
     finish_gather(0, 0)
     start_gather(0, 1)
-    permute_columns(3, SAME // 256)
-    start(column_exchange)
+    permute_columns(4, SAME // 256)
     finish_gather(0, 1)
     start_gather(0, 2)
+    start(column_exchange)
 
     for copy in block_copies[:3]:
         copy.wait()
@@ -557,7 +561,7 @@
             pltpu.VMEM((3, 8, 8, K), F32),
             dma((L,)), dma((L,)), dma((6,)), dma((2,)), dma((2, L)),
             dma((4, 2)), dma((4, 2)), dma((2, 2, 3, 3)), dma((2, 2, 3, 3)),
-            dma((1,)), dma((1,)), dma((2,)), dma((2,)), dma((4,)), dma((4,)),
+            dma((1,)), dma((1,)), dma((2,)), dma((2,)), dma((2,)), dma((2,)),
             dma((2,)), dma((2,)), dma((3, 7)), dma((3, 7)),
         ],
         compiler_params=pltpu.CompilerParams(

time: 79.4 us -> 76.3 us (0.961)
  Pallas kernels: 78.7 us -> 75.5 us
    pallas_call x1, Pallas kernels: 73 us -> 69.9 us  [local(): pl.pallas_call(kernel, out_shape=outs, in_specs=[hbm] * 8, out_specs=(hbm...]
where the time goes in v4:
time: 76.3 us; the launch traced here: 76.2 us
  Pallas kernels  75.5 us (99%)
    pallas_call x1, Pallas kernels, local(): pl.pallas_call(kernel, out_shape=outs, in_specs=[hbm] * 8, out_specs=(hbm...  69.9 us
    pallas_call x1, Pallas kernels, local(): pl.pallas_call(deliver, out_shape=outs, in_specs=[hbm] * 3, out_specs=(hb...  5.63 us

profile of v4, /device:TPU:0, one launch (start us, length us, event | category | flops | bytes accessed | tf_op | source)
XLA Modules:
  0.0 76.2 jit_solution(13121150266781108683)
XLA Ops:
  0.6 69.9 %shard_map.103 = (f32[8,256,384]{2,1,0:T(8,128)}, f32[8,256,384]{2,1,0:T(8,128)}, f32[1,256]{1,0:T(1,128)}) custom-call(f32[8,256,384]{2,1,0:T(8,128)} %loads_h.1, bf16[8,384,384]{2,1,0:T(8,128)(2,1)} %diagonal_h.1, bf16[8,384,384]{2,1,0:T(8,128)(2,1)} %lower_h.1, bf16[8,384,384]{2,1,0:T(8,128)(2,1)} %upper_h.1, bf16[3,8,384,384]{3,2,1,0:T(8,128)(2,1)} %local_h.1, ...), custom_call_target="tpu_custom_call" | custom-call | flops 8000000000 | bytes 25000000 | tf_op jit(solution)/shard_map/pallas_call | solution.py:532
  70.6 5.6 %shard_map.104 = (f32[8,256,384]{2,1,0:T(8,128)}, f32[8,256,384]{2,1,0:T(8,128)}, f32[1,256]{1,0:T(1,128)}) custom-call(f32[8,256,384]{2,1,0:T(8,128)} %get-tuple-element.9.answer, f32[8,256,384]{2,1,0:T(8,128)} %get-tuple-element.10.residual, f32[1,256]{1,0:T(1,128)} %get-tuple-element.11.relative), custom_call_target="tpu_custom_call" | custom-call | tf_op jit(solution)/shard_map/pallas_call | solution.py:577

commit v5 on v4

--- a/solution.py
+++ b/solution.py
@@ -354,9 +354,9 @@
     finish_gather(0, 0)
     start_gather(0, 1)
     permute_columns(4, SAME // 256)
+    start(column_exchange)
     finish_gather(0, 1)
     start_gather(0, 2)
-    start(column_exchange)
 
     for copy in block_copies[:3]:
         copy.wait()

time: 76.3 us -> 76.3 us (level)
  no operation moved by 1% of the time
where the time goes in v5:
time: 76.3 us; the launch traced here: 76.1 us
  Pallas kernels  75.5 us (99%)
    pallas_call x1, Pallas kernels, local(): pl.pallas_call(kernel, out_shape=outs, in_specs=[hbm] * 8, out_specs=(hbm...  69.9 us
    pallas_call x1, Pallas kernels, local(): pl.pallas_call(deliver, out_shape=outs, in_specs=[hbm] * 3, out_specs=(hb...  5.63 us

profile of v5, /device:TPU:0, one launch (start us, length us, event | category | flops | bytes accessed | tf_op | source)
XLA Modules:
  0.0 76.1 jit_solution(16543247796815803287)
XLA Ops:
  0.6 69.9 %shard_map.103 = (f32[8,256,384]{2,1,0:T(8,128)}, f32[8,256,384]{2,1,0:T(8,128)}, f32[1,256]{1,0:T(1,128)}) custom-call(f32[8,256,384]{2,1,0:T(8,128)} %loads_h.1, bf16[8,384,384]{2,1,0:T(8,128)(2,1)} %diagonal_h.1, bf16[8,384,384]{2,1,0:T(8,128)(2,1)} %lower_h.1, bf16[8,384,384]{2,1,0:T(8,128)(2,1)} %upper_h.1, bf16[3,8,384,384]{3,2,1,0:T(8,128)(2,1)} %local_h.1, ...), custom_call_target="tpu_custom_call" | custom-call | flops 8000000000 | bytes 25000000 | tf_op jit(solution)/shard_map/pallas_call | solution.py:532
  70.5 5.6 %shard_map.104 = (f32[8,256,384]{2,1,0:T(8,128)}, f32[8,256,384]{2,1,0:T(8,128)}, f32[1,256]{1,0:T(1,128)}) custom-call(f32[8,256,384]{2,1,0:T(8,128)} %get-tuple-element.9.answer, f32[8,256,384]{2,1,0:T(8,128)} %get-tuple-element.10.residual, f32[1,256]{1,0:T(1,128)} %get-tuple-element.11.relative), custom_call_target="tpu_custom_call" | custom-call | tf_op jit(solution)/shard_map/pallas_call | solution.py:577
